TPU v7x, 128 devices: a whole 4x4x4 slice. The times are simulated.
128 devices in a mesh: row: 16 (over y_hi, x, core), col: 8 (over y_lo, z).
Axes of the slice: x: 4, y: 4 (y_hi: 2, y_lo: 2; y = y_hi * 2 + y_lo), z: 4, core: 2. Of those that a mesh axis runs over, the one named last changes fastest.
Arguments:
- stem: float32 [2, 16, 8, 4, 256, 256], P(None, 'row', 'col'), may hold values from -6 to 6
- branch_one: float32 [2, 256, 256], replicated, may hold values from -0.25 to 0.25
- branch_two: float32 [2, 256, 256], replicated, may hold values from -0.25 to 0.25
- branch_three: float32 [2, 256, 256], replicated, may hold values from -0.25 to 0.25
- branch_four: float32 [2, 256, 256], replicated, may hold values from -0.25 to 0.25
- relabel: int32 [256], replicated, may hold values from 0 to 255, each once
Outputs:
- amplitudes: float32 [2, 8, 256, 256], P(None, None, 'col', 'row')
Inputs may be any that keep to these rules, and one draw needn't show every extreme that they name: `relabel`: each of the 256 values appears once.
All inputs are finite; a program needn't handle non-finite values.
Results may differ from a plain program's by a relative error of at most 0.00007.
Values sent between devices are 32-bit elements; how exact they have to be, the bound alone decides.
A program may use at most 128 MiB of HBM per device.

v0:
```python
import functools

import jax
import jax.numpy as jnp
from jax import lax
from jax.experimental import pallas as pl
from jax.experimental.pallas import tpu as pltpu
from jax.sharding import PartitionSpec as P

MESH = pl.DeviceIdType.MESH
F32, BF16 = jnp.float32, jnp.bfloat16
NT = (((1,), (1,)), ((), ()))
NN = (((1,), (0,)), ((), ()))

OFFSETS = ((1, 2), (1, 1), (1, 3), (0, 2), (1, 0), (0, 1), (0, 3), (0, 0))
PIECES = 4


def dot(lhs, rhs, dims):
    return lax.dot_general(lhs, rhs, dims, preferred_element_type=F32)


def split(value):
    high = value.astype(BF16)
    return high, (value - high.astype(F32)).astype(BF16)


def hops(offset):
    return offset[0] + min(offset[1], 4 - offset[1])


def shifted(index, offset, sign):
    high, low = index // 4, index % 4
    return ((high + 2 + sign * offset[0]) % 2) * 4 + (low + 4 + sign * offset[1]) % 4


def lanes_to(value, source, target):
    amount = (target - source) * 32 % 128
    return value if amount == 0 else pltpu.roll(value, amount, value.ndim - 1)


def regroup(tiles, lane_group):
    out = []
    for j in range(4):
        made = lanes_to(tiles[0], j, 0)
        for i in range(1, 4):
            made = jnp.where(lane_group == i, lanes_to(tiles[i], j, i), made)
        out.append(made)
    return out


def put_left(ref, real_part, imag_part, rows, width, row=0, column=0):
    parts = list(zip(split(real_part), split(imag_part)))
    for block, (re, im) in enumerate((parts[0], parts[1], parts[0])):
        at = column + block * 2 * width
        ref[row : row + rows, at : at + width] = re
        ref[row : row + rows, at + width : at + 2 * width] = -im
        ref[row + rows : row + 2 * rows, at : at + width] = im
        ref[row + rows : row + 2 * rows, at + width : at + 2 * width] = re


def kernel(
    factor, stem, one, two, three, four, relabel, out,
    stem_v, one_v, two_v, three_v, four_v, relabel_v,
    k_lhs, m_rhs, m_lhs, t_rhs, o_lhs, s_rhs, f_h, f_l,
    w_out, w_in, packed, landed, sums,
    stem_sem, one_sem, two_sem, three_sem, four_sem, relabel_sem,
    core_send, core_recv, far_send, far_recv, met, all_met,
):
    row, col = lax.axis_index("row"), lax.axis_index("col")
    chip, core = row // 2, row % 2
    partner = (chip * 2 + 1 - core, col)
    row_to = [shifted(chip, o, 1) for o in OFFSETS]
    col_to = [shifted(col, o, 1) for o in OFFSETS]
    col_from = [shifted(col, o, -1) for o in OFFSETS]
    order = sorted(
        ((j, k) for j in range(8) for k in range(8) if (j, k) != (7, 7)),
        key=lambda jk: -hops(OFFSETS[jk[0]]) - hops(OFFSETS[jk[1]]),
    )

    pltpu.make_async_copy(relabel, relabel_v, relabel_sem).start()
    column = pl.multiple_of(row // 8 * 128, 128)
    pltpu.make_async_copy(three.at[:, :, :, pl.ds(column, 128)], three_v, three_sem).start()
    for j in range(8):
        for half in range(2):
            source = 1 - core if half == 0 else core
            pltpu.make_async_copy(two.at[:, row_to[j], source], two_v.at[half, :, j], two_sem).start()
    for k in range(8):
        pltpu.make_async_copy(one.at[:, col_to[k]], one_v.at[:, k], one_sem).start()
    for u in range(2):
        for c in range(2):
            for f in range(4):
                pltpu.make_async_copy(
                    stem.at[c, f, u * 128 : u * 128 + 128], stem_v.at[u, c, f], stem_sem.at[u]
                ).start()

    barrier = pltpu.get_barrier_semaphore()

    @pl.when(core == 1)
    def _():
        pl.semaphore_signal(barrier, inc=1, device_id=partner, device_id_type=MESH)

    @pl.when(core == 0)
    def _():
        pl.semaphore_wait(barrier, 1)
        pl.semaphore_signal(met, inc=1, device_id=partner, device_id_type=MESH)

    @pl.when(core == 1)
    def _():
        pl.semaphore_wait(met, 1)
        for j, k in order:
            pl.semaphore_signal(barrier, inc=1, device_id=(row_to[j] * 2 + 1, col_to[k]), device_id_type=MESH)

    pltpu.make_async_copy(three_v, three_v, three_sem).wait()
    lane = lax.broadcasted_iota(jnp.int32, (16, 128), 1)
    turned = (128 - row % 8 * 16) % 128
    diagonal = (
        lax.broadcasted_iota(jnp.int32, (128, 128), 0) // 16 == lax.broadcasted_iota(jnp.int32, (128, 128), 1) // 16
    )
    block = []
    for c in range(2):
        piece = three_v[c, 0]
        for x in range(1, 16):
            piece = piece + three_v[c, x]
        piece = jnp.where(lane < 16, pltpu.roll(piece * factor, turned, 1), 0.0)
        for amount in (16, 32, 64):
            piece = piece + pltpu.roll(piece, amount, 1)
        block.append(jnp.where(diagonal, jnp.concatenate([piece] * 8, axis=0), 0.0))
    put_left(k_lhs, block[0], block[1], 128, 128)

    pltpu.make_async_copy(relabel_v, relabel_v, relabel_sem).wait()
    names = jnp.broadcast_to(relabel_v[...].reshape(1, 256), (256, 256))
    pick = jnp.where(lax.broadcasted_iota(jnp.int32, (256, 256), 0) == names, 1.0, 0.0).astype(BF16)
    pltpu.make_async_copy(two_v, two_v, two_sem).wait()
    for half in range(2):
        high, low = (dot(part, pick, NT).astype(BF16) for part in split(two_v[half].reshape(256, 256)))
        for block_at, part in enumerate((high, high, low)):
            m_rhs[block_at * 256 : block_at * 256 + 256, half * 256 : half * 256 + 256] = part
    m_all = dot(k_lhs[...], m_rhs[...], NN)
    for half in range(2):
        at = half * 256
        put_left(m_lhs, m_all[0:128, at : at + 256], m_all[128:256, at : at + 256], 128, 256, half * 256)

    pltpu.make_async_copy(one_v, one_v, one_sem).wait()
    for u in range(2):
        re, im = (one_v[c].reshape(256, 256)[:, u * 128 : u * 128 + 128] for c in range(2))
        put_left(o_lhs, re, im, 256, 128, 0, u * 768)
    first = None
    for u in range(2):
        pltpu.make_async_copy(stem_v.at[u], stem_v.at[u], stem_sem.at[u]).wait()
        for c in range(2):
            high, low = split((stem_v[u, c, 0] + stem_v[u, c, 1]) + (stem_v[u, c, 2] + stem_v[u, c, 3]))
            for block_at, part in enumerate((high, high, low)):
                at = u * 768 + block_at * 256 + c * 128
                t_rhs[at : at + 128] = part
        part = dot(o_lhs[:, u * 768 : u * 768 + 768], t_rhs[u * 768 : u * 768 + 768], NN)
        first = part if first is None else first + part
    for c in range(2):
        high, low = split(first[c * 256 : c * 256 + 256])
        for block_at, part in enumerate((high, high, low)):
            at = block_at * 512 + c * 256
            s_rhs[:, at : at + 256] = part
    pltpu.make_async_copy(four, four_v, four_sem).start()

    rows = 128 // PIECES
    w_out[...] = dot(m_lhs[0:256], s_rhs[...], NT).reshape(2, 128, 256)

    def core_copy(p):
        return pltpu.make_async_remote_copy(
            src_ref=w_out.at[:, p * rows : (p + 1) * rows],
            dst_ref=w_in.at[:, p * rows : (p + 1) * rows],
            send_sem=core_send.at[p],
            recv_sem=core_recv.at[p],
            device_id=partner,
            device_id_type=MESH,
        )

    for p in range(PIECES):
        core_copy(p).start()
    mine = dot(m_lhs[256:512], s_rhs[...], NT).reshape(2, 128, 256)

    @pl.when(core == 1)
    def _():
        pl.semaphore_wait(barrier, 63)
        pl.semaphore_signal(all_met, inc=1, device_id=partner, device_id_type=MESH)

    @pl.when(core == 0)
    def _():
        pl.semaphore_wait(all_met, 1)

    chips = 8 // PIECES
    groups = lax.broadcasted_iota(jnp.int32, (chips, 8, 128), 2) // 32
    for p in range(PIECES):
        core_copy(p).wait_recv()
        added = mine[:, p * rows : (p + 1) * rows] + w_in[:, p * rows : (p + 1) * rows]
        added = added.reshape(2, chips, 2, 8, 256)
        for h in range(2):
            tiles = [added[g // 2, :, g % 2, :, h * 128 : h * 128 + 128] for g in range(4)]
            for q, made in enumerate(regroup(tiles, groups)):
                packed[p * chips : (p + 1) * chips, h * 4 + q] = made
        for j, k in order:
            if j // chips == p:
                pltpu.make_async_remote_copy(
                    src_ref=packed.at[j, k],
                    dst_ref=landed.at[j * 8 + k],
                    send_sem=far_send,
                    recv_sem=far_recv,
                    device_id=(row_to[j] * 2 + core, col_to[k]),
                    device_id_type=MESH,
                ).start()

    pltpu.make_async_copy(four_v, four_v, four_sem).wait()
    for c in range(2):
        f_h[c * 256 : c * 256 + 256], f_l[c * 256 : c * 256 + 256] = split(four_v[c])

    pltpu.make_async_copy(landed.at[0:63], landed.at[0:63], far_recv).wait()
    for k in range(8):
        total = landed[k]
        for j in range(1, 7):
            total = total + landed[j * 8 + k]
        total = total + (landed[56 + k] if k < 7 else packed[7, 7])
        sums[col_from[k]] = total
    group = lax.broadcasted_iota(jnp.int32, (8, 128), 1) // 32
    v = jnp.concatenate(
        [jnp.concatenate(regroup([sums[h * 4 + q] for q in range(4)], group), axis=0) for h in range(2)], axis=1
    )
    v_h, v_l = split(v)
    first = dot(jnp.concatenate([v_h, v_l], axis=0), f_h[...], NT)
    made = first[0:32] + first[32:64] + dot(v_h, f_l[...], NT)
    result = (made[0:16, 0:256] - made[16:32, 256:512], made[0:16, 256:512] + made[16:32, 0:256])
    for c in range(2):
        for b in range(8):
            out[c, b] = result[c][:, b * 32 : b * 32 + 32]

    for p in range(PIECES):
        core_copy(p).wait_send()
    pltpu.make_async_copy(landed.at[0:63], landed.at[0:63], far_send).wait()


def body(stem, branch_one, branch_two, branch_three, branch_four, relabel):
    factor = (stem.shape[3] * lax.axis_size("row")) ** (-0.5)
    any_space = pl.BlockSpec(memory_space=pltpu.HBM)
    dma = pltpu.SemaphoreType.DMA
    made = pl.pallas_call(
        functools.partial(kernel, factor),
        out_shape=pltpu.VMEM((2, 8, 16, 32), F32),
        in_specs=[any_space] * 6,
        out_specs=pl.BlockSpec(memory_space=pltpu.VMEM),
        scratch_shapes=[
            pltpu.VMEM((2, 2, 4, 128, 256), F32),
            pltpu.VMEM((2, 8, 32, 256), F32),
            pltpu.VMEM((2, 2, 8, 16, 256), F32),
            pltpu.VMEM((2, 16, 16, 128), F32),
            pltpu.VMEM((2, 256, 256), F32),
            pltpu.VMEM((256,), jnp.int32),
            pltpu.VMEM((256, 768), BF16),
            pltpu.VMEM((768, 512), BF16),
            pltpu.VMEM((512, 1536), BF16),
            pltpu.VMEM((1536, 256), BF16),
            pltpu.VMEM((512, 1536), BF16),
            pltpu.VMEM((256, 1536), BF16),
            pltpu.VMEM((512, 256), BF16),
            pltpu.VMEM((512, 256), BF16),
            pltpu.VMEM((2, 128, 256), F32),
            pltpu.VMEM((2, 128, 256), F32),
            pltpu.VMEM((8, 8, 8, 128), F32),
            pltpu.VMEM((64, 8, 128), F32),
            pltpu.VMEM((8, 8, 128), F32),
            dma((2,)), dma, dma, dma, dma, dma,
            dma((PIECES,)), dma((PIECES,)), dma, dma,
            pltpu.SemaphoreType.REGULAR, pltpu.SemaphoreType.REGULAR,
        ],
        compiler_params=pltpu.CompilerParams(
            collective_id=0, has_side_effects=True, vmem_limit_bytes=40 << 20
        ),
        name="contract",
    )(
        *(
            pltpu.with_memory_space_constraint(value, pltpu.HBM)
            for value in (
                stem.reshape(2, 4, 256, 256),
                branch_one.reshape(2, 8, 32, 256),
                branch_two.reshape(2, 8, 2, 16, 256),
                branch_three.reshape(2, 16, 16, 256),
                branch_four,
                relabel,
            )
        )
    )
    return made.transpose(0, 1, 3, 2)


def solution(mesh):
    in_specs = (P(None, "row", "col", None, None, None), P(), P(), P(), P(), P())
    out_specs = P(None, None, "col", "row")
    return jax.shard_map(body, mesh=mesh, in_specs=in_specs, out_specs=out_specs, check_vma=False)
```

profile of v0, /device:TPU:1, one launch (start us, length us, event | category | flops | bytes accessed | tf_op | source)
XLA Modules:
  0.0 19.5 jit_solution(6037950604173471264)
XLA Ops:
  0.0 18.8 %contract.1 = f32[2,8,16,32]{3,2,1,0:T(8,128)S(1)} custom-call(f32[2,4,256,256]{3,2,1,0:T(8,128)} %bitcast.6, f32[2,8,32,256]{3,2,1,0:T(8,128)} %bitcast.7, f32[2,8,2,16,256]{4,3,2,1,0:T(8,128)} %bitcast.8, f32[2,16,16,256]{3,2,1,0:T(8,128)} %bitcast.9, f32[2,256,256]{2,1,0:T(8,128)} %four.1, s32[256]{0:T(256)} %relabel.1), custom_call_target="tpu_custom_call" | custom-call | tf_op jit(solution)/shard_map/contract/pallas_call | solution.py:244
  18.9 0.7 %copy.8 = f32[2,8,32,16]{2,3,1,0:T(8,128)} copy(f32[2,8,32,16]{2,3,1,0:T(8,128)S(1)} %bitcast.5) | data formatting | bytes 65536
where the time goes:
time: 19.6 us; the launch traced here: 19.5 us
  Pallas kernels  18.8 us (96%)
  local copies, waits for them, and re-layouts  0.66 us (3%)
    pallas_call x1, Pallas kernels, body(): pl.pallas_call(functools.partial(kernel, factor), out_shape=pltpu.VMEM((2...  18.8 us
    unnamed x1, local copies, waits for them, and re-layouts  0.66 us

commit v1 on v0

--- a/solution.py
+++ b/solution.py
@@ -50,13 +50,27 @@
 
 
 def put_left(ref, real_part, imag_part, rows, width, row=0, column=0):
-    parts = list(zip(split(real_part), split(imag_part)))
-    for block, (re, im) in enumerate((parts[0], parts[1], parts[0])):
+    for block, (re, im) in enumerate(zip(split(real_part), split(imag_part))):
         at = column + block * 2 * width
         ref[row : row + rows, at : at + width] = re
         ref[row : row + rows, at + width : at + 2 * width] = -im
         ref[row + rows : row + 2 * rows, at : at + width] = im
         ref[row + rows : row + 2 * rows, at + width : at + 2 * width] = re
+
+
+def three_dots(left_high, left_low, right_high, right_low, dims):
+    return dot(left_high, right_high, dims) + dot(left_low, right_high, dims) + dot(left_high, right_low, dims)
+
+
+def put_three(ref, real_part, imag_part):
+    for i, value in enumerate((real_part, imag_part, real_part + imag_part)):
+        for part, made in enumerate(split(value)):
+            ref[i, part] = made
+
+
+def product(left, right, dims):
+    rr, ii, ss = (three_dots(left[i, 0], left[i, 1], right[i, 0], right[i, 1], dims) for i in range(3))
+    return rr - ii, ss - rr - ii
 
 
 def kernel(
@@ -80,19 +94,17 @@
 
     pltpu.make_async_copy(relabel, relabel_v, relabel_sem).start()
     column = pl.multiple_of(row // 8 * 128, 128)
-    pltpu.make_async_copy(three.at[:, :, :, pl.ds(column, 128)], three_v, three_sem).start()
+    for x in range(16):
+        pltpu.make_async_copy(three.at[:, x, :, pl.ds(column, 128)], three_v.at[:, x], three_sem).start()
     for j in range(8):
         for half in range(2):
             source = 1 - core if half == 0 else core
             pltpu.make_async_copy(two.at[:, row_to[j], source], two_v.at[half, :, j], two_sem).start()
     for k in range(8):
         pltpu.make_async_copy(one.at[:, col_to[k]], one_v.at[:, k], one_sem).start()
-    for u in range(2):
-        for c in range(2):
-            for f in range(4):
-                pltpu.make_async_copy(
-                    stem.at[c, f, u * 128 : u * 128 + 128], stem_v.at[u, c, f], stem_sem.at[u]
-                ).start()
+    for c in range(2):
+        for f in range(0, 4, 2):
+            pltpu.make_async_copy(stem.at[c, f : f + 2], stem_v.at[c, f : f + 2], stem_sem).start()
 
     barrier = pltpu.get_barrier_semaphore()
 
@@ -134,36 +146,27 @@
     pltpu.make_async_copy(two_v, two_v, two_sem).wait()
     for half in range(2):
         high, low = (dot(part, pick, NT).astype(BF16) for part in split(two_v[half].reshape(256, 256)))
-        for block_at, part in enumerate((high, high, low)):
+        for block_at, part in enumerate((high, low)):
             m_rhs[block_at * 256 : block_at * 256 + 256, half * 256 : half * 256 + 256] = part
-    m_all = dot(k_lhs[...], m_rhs[...], NN)
-    for half in range(2):
-        at = half * 256
-        put_left(m_lhs, m_all[0:128, at : at + 256], m_all[128:256, at : at + 256], 128, 256, half * 256)
+    m_all = three_dots(k_lhs[:, 0:256], k_lhs[:, 256:512], m_rhs[0:256], m_rhs[256:512], NN)
+    stacked = [
+        jnp.concatenate([m_all[c * 128 : c * 128 + 128, 0:256], m_all[c * 128 : c * 128 + 128, 256:512]], axis=0)
+        for c in range(2)
+    ]
+    put_three(m_lhs, *stacked)
 
     pltpu.make_async_copy(one_v, one_v, one_sem).wait()
-    for u in range(2):
-        re, im = (one_v[c].reshape(256, 256)[:, u * 128 : u * 128 + 128] for c in range(2))
-        put_left(o_lhs, re, im, 256, 128, 0, u * 768)
-    first = None
-    for u in range(2):
-        pltpu.make_async_copy(stem_v.at[u], stem_v.at[u], stem_sem.at[u]).wait()
-        for c in range(2):
-            high, low = split((stem_v[u, c, 0] + stem_v[u, c, 1]) + (stem_v[u, c, 2] + stem_v[u, c, 3]))
-            for block_at, part in enumerate((high, high, low)):
-                at = u * 768 + block_at * 256 + c * 128
-                t_rhs[at : at + 128] = part
-        part = dot(o_lhs[:, u * 768 : u * 768 + 768], t_rhs[u * 768 : u * 768 + 768], NN)
-        first = part if first is None else first + part
-    for c in range(2):
-        high, low = split(first[c * 256 : c * 256 + 256])
-        for block_at, part in enumerate((high, high, low)):
-            at = block_at * 512 + c * 256
-            s_rhs[:, at : at + 256] = part
+    put_three(o_lhs, one_v[0].reshape(256, 256), one_v[1].reshape(256, 256))
+    pltpu.make_async_copy(stem_v, stem_v, stem_sem).wait()
+    put_three(t_rhs, *((stem_v[c, 0] + stem_v[c, 1]) + (stem_v[c, 2] + stem_v[c, 3]) for c in range(2)))
+    put_three(s_rhs, *product(o_lhs, t_rhs, NN))
     pltpu.make_async_copy(four, four_v, four_sem).start()
 
     rows = 128 // PIECES
-    w_out[...] = dot(m_lhs[0:256], s_rhs[...], NT).reshape(2, 128, 256)
+    w_parts = product(m_lhs, s_rhs, NT)
+    for c in range(2):
+        w_out[c] = w_parts[c][0:128]
+    mine = jnp.stack([w_parts[c][128:256] for c in range(2)])
 
     def core_copy(p):
         return pltpu.make_async_remote_copy(
@@ -177,7 +180,6 @@
 
     for p in range(PIECES):
         core_copy(p).start()
-    mine = dot(m_lhs[256:512], s_rhs[...], NT).reshape(2, 128, 256)
 
     @pl.when(core == 1)
     def _():
@@ -247,18 +249,15 @@
         in_specs=[any_space] * 6,
         out_specs=pl.BlockSpec(memory_space=pltpu.VMEM),
         scratch_shapes=[
-            pltpu.VMEM((2, 2, 4, 128, 256), F32),
+            pltpu.VMEM((2, 4, 256, 256), F32),
             pltpu.VMEM((2, 8, 32, 256), F32),
             pltpu.VMEM((2, 2, 8, 16, 256), F32),
             pltpu.VMEM((2, 16, 16, 128), F32),
             pltpu.VMEM((2, 256, 256), F32),
             pltpu.VMEM((256,), jnp.int32),
-            pltpu.VMEM((256, 768), BF16),
-            pltpu.VMEM((768, 512), BF16),
-            pltpu.VMEM((512, 1536), BF16),
-            pltpu.VMEM((1536, 256), BF16),
-            pltpu.VMEM((512, 1536), BF16),
-            pltpu.VMEM((256, 1536), BF16),
+            pltpu.VMEM((256, 512), BF16),
+            pltpu.VMEM((512, 512), BF16),
+            *[pltpu.VMEM((3, 2, 256, 256), BF16)] * 4,
             pltpu.VMEM((512, 256), BF16),
             pltpu.VMEM((512, 256), BF16),
             pltpu.VMEM((2, 128, 256), F32),
@@ -266,7 +265,7 @@
             pltpu.VMEM((8, 8, 8, 128), F32),
             pltpu.VMEM((64, 8, 128), F32),
             pltpu.VMEM((8, 8, 128), F32),
-            dma((2,)), dma, dma, dma, dma, dma,
+            dma, dma, dma, dma, dma, dma,
             dma((PIECES,)), dma((PIECES,)), dma, dma,
             pltpu.SemaphoreType.REGULAR, pltpu.SemaphoreType.REGULAR,
         ],

time: 19.6 us -> 18.2 us (0.929)
  Pallas kernels: 18.8 us -> 17.4 us
    pallas_call x1, Pallas kernels: 18.8 us -> 17.4 us  [body(): pl.pallas_call(functools.partial(kernel, factor), out_shape=pltpu.VMEM((2...]
where the time goes in v1:
time: 18.2 us; the launch traced here: 18.1 us
  Pallas kernels  17.4 us (96%)
  local copies, waits for them, and re-layouts  0.66 us (4%)
    pallas_call x1, Pallas kernels, body(): pl.pallas_call(functools.partial(kernel, factor), out_shape=pltpu.VMEM((2...  17.4 us
    unnamed x1, local copies, waits for them, and re-layouts  0.66 us

profile of v1, /device:TPU:1, one launch (start us, length us, event | category | flops | bytes accessed | tf_op | source)
XLA Modules:
  0.0 18.1 jit_solution(17732054217650251174)
XLA Ops:
  0.0 17.4 %contract.1 = f32[2,8,16,32]{3,2,1,0:T(8,128)S(1)} custom-call(f32[2,4,256,256]{3,2,1,0:T(8,128)} %bitcast.6, f32[2,8,32,256]{3,2,1,0:T(8,128)} %bitcast.7, f32[2,8,2,16,256]{4,3,2,1,0:T(8,128)} %bitcast.8, f32[2,16,16,256]{3,2,1,0:T(8,128)} %bitcast.9, f32[2,256,256]{2,1,0:T(8,128)} %four.1, s32[256]{0:T(256)} %relabel.1), custom_call_target="tpu_custom_call" | custom-call | tf_op jit(solution)/shard_map/contract/pallas_call | solution.py:246
  17.4 0.7 %copy.8 = f32[2,8,32,16]{2,3,1,0:T(8,128)} copy(f32[2,8,32,16]{2,3,1,0:T(8,128)S(1)} %bitcast.5) | data formatting | bytes 65536

commit v2 on v1

--- a/solution.py
+++ b/solution.py
@@ -25,8 +25,9 @@
     return high, (value - high.astype(F32)).astype(BF16)
 
 
-def hops(offset):
-    return offset[0] + min(offset[1], 4 - offset[1])
+def hops(j, k):
+    (y_hi, x), (y_lo, z) = OFFSETS[j], OFFSETS[k]
+    return min(x, 4 - x) + min(z, 4 - z) + (1 if y_lo else 2 * y_hi)
 
 
 def shifted(index, offset, sign):
@@ -89,8 +90,14 @@
     col_from = [shifted(col, o, -1) for o in OFFSETS]
     order = sorted(
         ((j, k) for j in range(8) for k in range(8) if (j, k) != (7, 7)),
-        key=lambda jk: -hops(OFFSETS[jk[0]]) - hops(OFFSETS[jk[1]]),
-    )
+        key=lambda jk: -hops(*jk),
+    )
+
+    barrier = pltpu.get_barrier_semaphore()
+
+    @pl.when(core == 1)
+    def _():
+        pl.semaphore_signal(barrier, inc=1, device_id=partner, device_id_type=MESH)
 
     pltpu.make_async_copy(relabel, relabel_v, relabel_sem).start()
     column = pl.multiple_of(row // 8 * 128, 128)
@@ -104,13 +111,7 @@
         pltpu.make_async_copy(one.at[:, col_to[k]], one_v.at[:, k], one_sem).start()
     for c in range(2):
         for f in range(0, 4, 2):
-            pltpu.make_async_copy(stem.at[c, f : f + 2], stem_v.at[c, f : f + 2], stem_sem).start()
-
-    barrier = pltpu.get_barrier_semaphore()
-
-    @pl.when(core == 1)
-    def _():
-        pl.semaphore_signal(barrier, inc=1, device_id=partner, device_id_type=MESH)
+            pltpu.make_async_copy(stem.at[c, f : f + 2], stem_v.at[c, f : f + 2], stem_sem).start(priority=1)
 
     @pl.when(core == 0)
     def _():

time: 18.2 us -> 17.3 us (0.951)
  Pallas kernels: 17.4 us -> 16.5 us
    pallas_call x1, Pallas kernels: 17.4 us -> 16.5 us  [body(): pl.pallas_call(functools.partial(kernel, factor), out_shape=pltpu.VMEM((2...]
where the time goes in v2:
time: 17.3 us; the launch traced here: 17.2 us
  Pallas kernels  16.5 us (95%)
  local copies, waits for them, and re-layouts  0.66 us (4%)
    pallas_call x1, Pallas kernels, body(): pl.pallas_call(functools.partial(kernel, factor), out_shape=pltpu.VMEM((2...  16.5 us
    unnamed x1, local copies, waits for them, and re-layouts  0.66 us

profile of v2, /device:TPU:1, one launch (start us, length us, event | category | flops | bytes accessed | tf_op | source)
XLA Modules:
  0.0 17.2 jit_solution(9843733296765587749)
XLA Ops:
  0.0 16.5 %contract.1 = f32[2,8,16,32]{3,2,1,0:T(8,128)S(1)} custom-call(f32[2,4,256,256]{3,2,1,0:T(8,128)} %bitcast.6, f32[2,8,32,256]{3,2,1,0:T(8,128)} %bitcast.7, f32[2,8,2,16,256]{4,3,2,1,0:T(8,128)} %bitcast.8, f32[2,16,16,256]{3,2,1,0:T(8,128)} %bitcast.9, f32[2,256,256]{2,1,0:T(8,128)} %four.1, s32[256]{0:T(256)} %relabel.1), custom_call_target="tpu_custom_call" | custom-call | tf_op jit(solution)/shard_map/contract/pallas_call | solution.py:247
  16.5 0.7 %copy.8 = f32[2,8,32,16]{2,3,1,0:T(8,128)} copy(f32[2,8,32,16]{2,3,1,0:T(8,128)S(1)} %bitcast.5) | data formatting | bytes 65536

commit v3 on v2

--- a/solution.py
+++ b/solution.py
@@ -12,8 +12,9 @@
 NT = (((1,), (1,)), ((), ()))
 NN = (((1,), (0,)), ((), ()))
 
-OFFSETS = ((1, 2), (1, 1), (1, 3), (0, 2), (1, 0), (0, 1), (0, 3), (0, 0))
+OFFSETS = ((1, 2), (1, 1), (1, 0), (1, 3), (0, 2), (0, 1), (0, 3), (0, 0))
 PIECES = 4
+LATE = 5
 
 
 def dot(lhs, rhs, dims):
@@ -78,7 +79,7 @@
     factor, stem, one, two, three, four, relabel, out,
     stem_v, one_v, two_v, three_v, four_v, relabel_v,
     k_lhs, m_rhs, m_lhs, t_rhs, o_lhs, s_rhs, f_h, f_l,
-    w_out, w_in, packed, landed, sums,
+    w_out, w_in, packed, landed,
     stem_sem, one_sem, two_sem, three_sem, four_sem, relabel_sem,
     core_send, core_recv, far_send, far_recv, met, all_met,
 ):
@@ -92,6 +93,8 @@
         ((j, k) for j in range(8) for k in range(8) if (j, k) != (7, 7)),
         key=lambda jk: -hops(*jk),
     )
+    x, y, z = chip % 4, chip // 4 * 2 + col // 4, col % 4
+    late = jnp.minimum(x, 4 - x) + jnp.minimum(y, 4 - y) + z >= LATE
 
     barrier = pltpu.get_barrier_semaphore()
 
@@ -103,6 +106,11 @@
     column = pl.multiple_of(row // 8 * 128, 128)
     for x in range(16):
         pltpu.make_async_copy(three.at[:, x, :, pl.ds(column, 128)], three_v.at[:, x], three_sem).start()
+    @pl.when(core == 0)
+    def _():
+        pl.semaphore_wait(barrier, 1)
+        pl.semaphore_signal(met, inc=1, device_id=partner, device_id_type=MESH)
+
     for j in range(8):
         for half in range(2):
             source = 1 - core if half == 0 else core
@@ -112,11 +120,6 @@
     for c in range(2):
         for f in range(0, 4, 2):
             pltpu.make_async_copy(stem.at[c, f : f + 2], stem_v.at[c, f : f + 2], stem_sem).start(priority=1)
-
-    @pl.when(core == 0)
-    def _():
-        pl.semaphore_wait(barrier, 1)
-        pl.semaphore_signal(met, inc=1, device_id=partner, device_id_type=MESH)
 
     @pl.when(core == 1)
     def _():
@@ -182,14 +185,27 @@
     for p in range(PIECES):
         core_copy(p).start()
 
-    @pl.when(core == 1)
-    def _():
-        pl.semaphore_wait(barrier, 63)
-        pl.semaphore_signal(all_met, inc=1, device_id=partner, device_id_type=MESH)
-
-    @pl.when(core == 0)
-    def _():
-        pl.semaphore_wait(all_met, 1)
+    def wait_for_far(condition):
+        @pl.when((core == 1) & condition)
+        def _():
+            pl.semaphore_wait(barrier, 63)
+            pl.semaphore_signal(all_met, inc=1, device_id=partner, device_id_type=MESH)
+
+        @pl.when((core == 0) & condition)
+        def _():
+            pl.semaphore_wait(all_met, 1)
+
+    def send(j, k):
+        pltpu.make_async_remote_copy(
+            src_ref=packed.at[j, k],
+            dst_ref=landed.at[j * 8 + k],
+            send_sem=far_send,
+            recv_sem=far_recv,
+            device_id=(row_to[j] * 2 + core, col_to[k]),
+            device_id_type=MESH,
+        ).start()
+
+    wait_for_far(late)
 
     chips = 8 // PIECES
     groups = lax.broadcasted_iota(jnp.int32, (chips, 8, 128), 2) // 32
@@ -201,35 +217,44 @@
             tiles = [added[g // 2, :, g % 2, :, h * 128 : h * 128 + 128] for g in range(4)]
             for q, made in enumerate(regroup(tiles, groups)):
                 packed[p * chips : (p + 1) * chips, h * 4 + q] = made
+
+        @pl.when(late)
+        def _():
+            for j, k in order:
+                if j // chips == p:
+                    send(j, k)
+
+    early = jnp.logical_not(late)
+    wait_for_far(early)
+
+    @pl.when(early)
+    def _():
         for j, k in order:
-            if j // chips == p:
-                pltpu.make_async_remote_copy(
-                    src_ref=packed.at[j, k],
-                    dst_ref=landed.at[j * 8 + k],
-                    send_sem=far_send,
-                    recv_sem=far_recv,
-                    device_id=(row_to[j] * 2 + core, col_to[k]),
-                    device_id_type=MESH,
-                ).start()
+            send(j, k)
 
     pltpu.make_async_copy(four_v, four_v, four_sem).wait()
-    for c in range(2):
-        f_h[c * 256 : c * 256 + 256], f_l[c * 256 : c * 256 + 256] = split(four_v[c])
+    low = lax.broadcasted_iota(jnp.int32, (32, 256), 0)
+    lane = lax.broadcasted_iota(jnp.int32, (32, 256), 1)
+    turn = jnp.concatenate([jnp.where(lane == low + col_from[k] * 32, 1.0, 0.0) for k in range(8)], axis=0).astype(BF16)
+    for c in range(2):
+        for ref, part in zip((f_h, f_l), split(four_v[c])):
+            ref[:, c * 256 : c * 256 + 256] = dot(turn, part, NT).astype(BF16)
 
     pltpu.make_async_copy(landed.at[0:63], landed.at[0:63], far_recv).wait()
+    totals = []
     for k in range(8):
         total = landed[k]
         for j in range(1, 7):
             total = total + landed[j * 8 + k]
         total = total + (landed[56 + k] if k < 7 else packed[7, 7])
-        sums[col_from[k]] = total
+        totals.append(total)
     group = lax.broadcasted_iota(jnp.int32, (8, 128), 1) // 32
     v = jnp.concatenate(
-        [jnp.concatenate(regroup([sums[h * 4 + q] for q in range(4)], group), axis=0) for h in range(2)], axis=1
+        [jnp.concatenate(regroup(totals[h * 4 : h * 4 + 4], group), axis=0) for h in range(2)], axis=1
     )
     v_h, v_l = split(v)
-    first = dot(jnp.concatenate([v_h, v_l], axis=0), f_h[...], NT)
-    made = first[0:32] + first[32:64] + dot(v_h, f_l[...], NT)
+    first = dot(jnp.concatenate([v_h, v_l], axis=0), f_h[...], NN)
+    made = first[0:32] + first[32:64] + dot(v_h, f_l[...], NN)
     result = (made[0:16, 0:256] - made[16:32, 256:512], made[0:16, 256:512] + made[16:32, 0:256])
     for c in range(2):
         for b in range(8):
@@ -259,13 +284,12 @@
             pltpu.VMEM((256, 512), BF16),
             pltpu.VMEM((512, 512), BF16),
             *[pltpu.VMEM((3, 2, 256, 256), BF16)] * 4,
-            pltpu.VMEM((512, 256), BF16),
-            pltpu.VMEM((512, 256), BF16),
+            pltpu.VMEM((256, 512), BF16),
+            pltpu.VMEM((256, 512), BF16),
             pltpu.VMEM((2, 128, 256), F32),
             pltpu.VMEM((2, 128, 256), F32),
             pltpu.VMEM((8, 8, 8, 128), F32),
             pltpu.VMEM((64, 8, 128), F32),
-            pltpu.VMEM((8, 8, 128), F32),
             dma, dma, dma, dma, dma, dma,
             dma((PIECES,)), dma((PIECES,)), dma, dma,
             pltpu.SemaphoreType.REGULAR, pltpu.SemaphoreType.REGULAR,

time: 17.3 us -> 17.2 us (level)
  no operation moved by 1% of the time
where the time goes in v3:
time: 17.2 us; the launch traced here: 17.1 us
  Pallas kernels  16.4 us (95%)
  local copies, waits for them, and re-layouts  0.66 us (4%)
    pallas_call x1, Pallas kernels, body(): pl.pallas_call(functools.partial(kernel, factor), out_shape=pltpu.VMEM((2...  16.4 us
    unnamed x1, local copies, waits for them, and re-layouts  0.66 us

profile of v3, /device:TPU:1, one launch (start us, length us, event | category | flops | bytes accessed | tf_op | source)
XLA Modules:
  0.0 17.1 jit_solution(2191231434282752600)
XLA Ops:
  0.0 16.4 %contract.1 = f32[2,8,16,32]{3,2,1,0:T(8,128)S(1)} custom-call(f32[2,4,256,256]{3,2,1,0:T(8,128)} %bitcast.6, f32[2,8,32,256]{3,2,1,0:T(8,128)} %bitcast.7, f32[2,8,2,16,256]{4,3,2,1,0:T(8,128)} %bitcast.8, f32[2,16,16,256]{3,2,1,0:T(8,128)} %bitcast.9, f32[2,256,256]{2,1,0:T(8,128)} %four.1, s32[256]{0:T(256)} %relabel.1), custom_call_target="tpu_custom_call" | custom-call | tf_op jit(solution)/shard_map/contract/pallas_call | solution.py:272
  16.4 0.7 %copy.8 = f32[2,8,32,16]{2,3,1,0:T(8,128)} copy(f32[2,8,32,16]{2,3,1,0:T(8,128)S(1)} %bitcast.5) | data formatting | bytes 65536

commit v4 on v3

--- a/solution.py
+++ b/solution.py
@@ -205,8 +205,6 @@
             device_id_type=MESH,
         ).start()
 
-    wait_for_far(late)
-
     chips = 8 // PIECES
     groups = lax.broadcasted_iota(jnp.int32, (chips, 8, 128), 2) // 32
     for p in range(PIECES):
@@ -217,6 +215,9 @@
             tiles = [added[g // 2, :, g % 2, :, h * 128 : h * 128 + 128] for g in range(4)]
             for q, made in enumerate(regroup(tiles, groups)):
                 packed[p * chips : (p + 1) * chips, h * 4 + q] = made
+
+        if p == 0:
+            wait_for_far(late)
 
         @pl.when(late)
         def _():

time: 17.2 us -> 17.1 us (level)
  no operation moved by 1% of the time
where the time goes in v4:
time: 17.1 us; the launch traced here: 16.9 us
  Pallas kernels  16.3 us (95%)
  local copies, waits for them, and re-layouts  0.66 us (4%)
    pallas_call x1, Pallas kernels, body(): pl.pallas_call(functools.partial(kernel, factor), out_shape=pltpu.VMEM((2...  16.3 us
    unnamed x1, local copies, waits for them, and re-layouts  0.66 us

profile of v4, /device:TPU:1, one launch (start us, length us, event | category | flops | bytes accessed | tf_op | source)
XLA Modules:
  0.0 16.9 jit_solution(9552639720135479441)
XLA Ops:
  0.0 16.3 %contract.1 = f32[2,8,16,32]{3,2,1,0:T(8,128)S(1)} custom-call(f32[2,4,256,256]{3,2,1,0:T(8,128)} %bitcast.6, f32[2,8,32,256]{3,2,1,0:T(8,128)} %bitcast.7, f32[2,8,2,16,256]{4,3,2,1,0:T(8,128)} %bitcast.8, f32[2,16,16,256]{3,2,1,0:T(8,128)} %bitcast.9, f32[2,256,256]{2,1,0:T(8,128)} %four.1, s32[256]{0:T(256)} %relabel.1), custom_call_target="tpu_custom_call" | custom-call | tf_op jit(solution)/shard_map/contract/pallas_call | solution.py:273
  16.3 0.7 %copy.8 = f32[2,8,32,16]{2,3,1,0:T(8,128)} copy(f32[2,8,32,16]{2,3,1,0:T(8,128)S(1)} %bitcast.5) | data formatting | bytes 65536

commit v5 on v2

--- a/solution.py
+++ b/solution.py
@@ -12,7 +12,7 @@
 NT = (((1,), (1,)), ((), ()))
 NN = (((1,), (0,)), ((), ()))
 
-OFFSETS = ((1, 2), (1, 1), (1, 3), (0, 2), (1, 0), (0, 1), (0, 3), (0, 0))
+OFFSETS = ((1, 2), (1, 1), (1, 0), (1, 3), (0, 2), (0, 1), (0, 3), (0, 0))
 PIECES = 4
 
 

time: 17.3 us -> 17.1 us (0.988)
  Pallas kernels: 16.5 us -> 16.3 us
    pallas_call x1, Pallas kernels: 16.5 us -> 16.3 us  [body(): pl.pallas_call(functools.partial(kernel, factor), out_shape=pltpu.VMEM((2...]
where the time goes in v5:
time: 17.1 us; the launch traced here: 17 us
  Pallas kernels  16.3 us (95%)
  local copies, waits for them, and re-layouts  0.66 us (4%)
    pallas_call x1, Pallas kernels, body(): pl.pallas_call(functools.partial(kernel, factor), out_shape=pltpu.VMEM((2...  16.3 us
    unnamed x1, local copies, waits for them, and re-layouts  0.66 us

profile of v5, /device:TPU:1, one launch (start us, length us, event | category | flops | bytes accessed | tf_op | source)
XLA Modules:
  0.0 17.0 jit_solution(10568484494987775153)
XLA Ops:
  0.0 16.3 %contract.1 = f32[2,8,16,32]{3,2,1,0:T(8,128)S(1)} custom-call(f32[2,4,256,256]{3,2,1,0:T(8,128)} %bitcast.6, f32[2,8,32,256]{3,2,1,0:T(8,128)} %bitcast.7, f32[2,8,2,16,256]{4,3,2,1,0:T(8,128)} %bitcast.8, f32[2,16,16,256]{3,2,1,0:T(8,128)} %bitcast.9, f32[2,256,256]{2,1,0:T(8,128)} %four.1, s32[256]{0:T(256)} %relabel.1), custom_call_target="tpu_custom_call" | custom-call | tf_op jit(solution)/shard_map/contract/pallas_call | solution.py:247
  16.3 0.7 %copy.8 = f32[2,8,32,16]{2,3,1,0:T(8,128)} copy(f32[2,8,32,16]{2,3,1,0:T(8,128)S(1)} %bitcast.5) | data formatting | bytes 65536

commit v6 on v5

--- a/solution.py
+++ b/solution.py
@@ -103,6 +103,11 @@
     column = pl.multiple_of(row // 8 * 128, 128)
     for x in range(16):
         pltpu.make_async_copy(three.at[:, x, :, pl.ds(column, 128)], three_v.at[:, x], three_sem).start()
+    @pl.when(core == 0)
+    def _():
+        pl.semaphore_wait(barrier, 1)
+        pl.semaphore_signal(met, inc=1, device_id=partner, device_id_type=MESH)
+
     for j in range(8):
         for half in range(2):
             source = 1 - core if half == 0 else core
@@ -112,11 +117,6 @@
     for c in range(2):
         for f in range(0, 4, 2):
             pltpu.make_async_copy(stem.at[c, f : f + 2], stem_v.at[c, f : f + 2], stem_sem).start(priority=1)
-
-    @pl.when(core == 0)
-    def _():
-        pl.semaphore_wait(barrier, 1)
-        pl.semaphore_signal(met, inc=1, device_id=partner, device_id_type=MESH)
 
     @pl.when(core == 1)
     def _():

time: 17.1 us -> 17.2 us (level)
  no operation moved by 1% of the time
where the time goes in v6:
time: 17.2 us; the launch traced here: 17.1 us
  Pallas kernels  16.4 us (95%)
  local copies, waits for them, and re-layouts  0.66 us (4%)
    pallas_call x1, Pallas kernels, body(): pl.pallas_call(functools.partial(kernel, factor), out_shape=pltpu.VMEM((2...  16.4 us
    unnamed x1, local copies, waits for them, and re-layouts  0.66 us

profile of v6, /device:TPU:1, one launch (start us, length us, event | category | flops | bytes accessed | tf_op | source)
XLA Modules:
  0.0 17.1 jit_solution(7283145327797080598)
XLA Ops:
  0.0 16.4 %contract.1 = f32[2,8,16,32]{3,2,1,0:T(8,128)S(1)} custom-call(f32[2,4,256,256]{3,2,1,0:T(8,128)} %bitcast.6, f32[2,8,32,256]{3,2,1,0:T(8,128)} %bitcast.7, f32[2,8,2,16,256]{4,3,2,1,0:T(8,128)} %bitcast.8, f32[2,16,16,256]{3,2,1,0:T(8,128)} %bitcast.9, f32[2,256,256]{2,1,0:T(8,128)} %four.1, s32[256]{0:T(256)} %relabel.1), custom_call_target="tpu_custom_call" | custom-call | tf_op jit(solution)/shard_map/contract/pallas_call | solution.py:247
  16.5 0.7 %copy.8 = f32[2,8,32,16]{2,3,1,0:T(8,128)} copy(f32[2,8,32,16]{2,3,1,0:T(8,128)S(1)} %bitcast.5) | data formatting | bytes 65536
